TPU v7x, 128 devices: a whole 4x4x4 slice. The times are simulated.
128 devices in a mesh: space: 32 (over z, x, core), head: 4 (over y).
Axes of the slice: x: 4, y: 4, z: 4, core: 2. Of those that a mesh axis runs over, the one named last changes fastest.
Arguments:
- tokens: bfloat16 [32768, 1024], P('space'), may hold values from -70 to 70
- w_qkv: bfloat16 [1024, 3, 1024], P(None, None, 'head'), may hold values from -7 to 7
- w_out: bfloat16 [1024, 1024], P('head'), may hold values from -0.5 to 0.5
- neighbours: int32 [256, 9], P('space'), may hold values from 0 to 71, as said below
- requests: int32 [32, 32, 2], P('space'), may hold values from -1 to 7, as said below
- cotangent: bfloat16 [32768, 1024], P('space', 'head'), may hold values from -6 to 6
Outputs:
- layer_out: bfloat16 [32768, 1024], P('space', 'head')
- grad_tokens: bfloat16 [32768, 1024], P('space', 'head')
- grad_w_qkv: float32 [1024, 3, 1024], P('space', None, 'head')
- grad_w_out: float32 [1024, 1024], P('head', 'space')
Inputs may be any that keep to these rules, and one draw needn't show every extreme that they name: `neighbours`: row t starts with t % 8 itself, then 3 other tiles of the same device, then 5 slot entries 8 + p * 2 + c; every slot entry names a filled request of that device, every filled request is named by some tile of that device, and no row names a tile twice. requests[d, p, c] is a tile of device p by its index within p, or -1 for an empty slot; filled slots come first and are distinct, requests[d, d] is empty, and in every draw some device fills all 2 slots towards some other device.
All inputs are finite; a program needn't handle non-finite values.
Results may differ from a plain program's by a relative error of at most 0.02.
The roundings to bfloat16 on the way count: a program that leaves them out, or rounds other values in their place, can miss the bound.
Values may be sent and summed in bfloat16 or wider, within the bound.
A program may use at most 192 MiB of HBM per device.

v0:
```python
import jax
import jax.numpy as jnp
from jax import lax
from jax.sharding import PartitionSpec as P

HEAD_DIM = 64
BLOCK_TILES = 4
NEIGHBOURS = 9
EPSILON = 1e-05


def norm_parts(tokens):
    values = tokens.astype(jnp.float32)
    centred = values - jnp.mean(values, axis=1, keepdims=True)
    inverse = lax.rsqrt(jnp.mean(centred * centred, axis=1, keepdims=True) + EPSILON)
    return (centred * inverse, inverse)


def gather_keys(extended, block_entries, head_count):
    entry_count = block_entries.shape[0]
    tile_rows = extended.shape[2]
    picked = jnp.take(extended, block_entries.reshape(-1), axis=1)
    return picked.reshape(2, entry_count, NEIGHBOURS * tile_rows, head_count, HEAD_DIM)


def probabilities(queries, key_part, score_scale):
    scores = (
        jnp.einsum("bihe,bjhe->bhij", queries, key_part, preferred_element_type=jnp.float32)
        * score_scale
    )
    row_top = jnp.max(scores, axis=3, keepdims=True)
    weights = jnp.exp(scores - row_top)
    return weights / jnp.sum(weights, axis=3, keepdims=True)


def select_pairs(local_pairs, incoming):
    peer_count, slot_count = incoming.shape
    flat_wanted = incoming.reshape(-1)
    usable = (flat_wanted >= 0)[None, :, None, None]
    picked = jnp.take(local_pairs, jnp.maximum(flat_wanted, 0), axis=1)
    picked = jnp.where(usable, picked, jnp.zeros_like(picked))
    return picked.reshape(2, peer_count, slot_count, local_pairs.shape[2], local_pairs.shape[3])


def on_device(tokens, w_qkv, w_out, neighbours, requests, cotangent):
    row_count, model_width = tokens.shape
    tile_count = neighbours.shape[0]
    tile_rows = row_count // tile_count
    head_width = w_qkv.shape[2]
    head_count = head_width // HEAD_DIM
    peer_count = lax.axis_size("space")
    slot_count = requests.shape[2]
    col_share = cotangent.shape[1]
    column = lax.axis_index("head") * col_share
    score_scale = HEAD_DIM ** (-0.5)
    block_count = tile_count // BLOCK_TILES
    extent = tile_count + peer_count * slot_count
    standard, inverse = norm_parts(tokens)
    normed = standard.astype(jnp.bfloat16)
    flat_weight = w_qkv.reshape(model_width, 3 * head_width)
    projected = jnp.dot(normed, flat_weight, preferred_element_type=jnp.float32).astype(
        jnp.bfloat16
    )
    queries = projected[:, :head_width].reshape(
        block_count, BLOCK_TILES, tile_rows, head_count, HEAD_DIM
    )
    local_pairs = jnp.transpose(
        projected[:, head_width:].reshape(row_count, 2, head_width), (1, 0, 2)
    )
    local_pairs = local_pairs.reshape(2, tile_count, tile_rows, head_width)
    entries = neighbours.reshape(block_count, BLOCK_TILES, NEIGHBOURS)
    incoming = lax.all_to_all(
        requests.reshape(peer_count, slot_count), "space", split_axis=0, concat_axis=0, tiled=True
    )
    outgoing = select_pairs(local_pairs, incoming)
    fetched, incoming = (
        lax.all_to_all(outgoing, "space", split_axis=1, concat_axis=1, tiled=True),
        incoming,
    )
    extended = jnp.concatenate(
        [local_pairs, fetched.reshape(2, peer_count * slot_count, tile_rows, head_width)], 1
    )

    def forward_block(inputs):
        block_queries, block_entries = inputs
        keyset = gather_keys(extended, block_entries, head_count)
        likely = probabilities(block_queries, keyset[0], score_scale)
        rounded = likely.astype(jnp.bfloat16)
        mixed = jnp.einsum(
            "bhij,bjhe->bihe", rounded, keyset[1], preferred_element_type=jnp.float32
        )
        return mixed.astype(jnp.bfloat16)

    attended = lax.map(forward_block, (queries, entries)).reshape(row_count, head_width)
    partial_out = jnp.dot(attended, w_out, preferred_element_type=jnp.float32)
    summed = lax.psum_scatter(
        partial_out.astype(jnp.bfloat16), "head", scatter_dimension=1, tiled=True
    ).astype(jnp.float32)
    own_tokens = lax.dynamic_slice_in_dim(tokens, column, col_share, 1).astype(jnp.float32)
    layer_out = (own_tokens + summed).astype(jnp.bfloat16)
    cotangent_full = lax.all_gather(cotangent, "head", axis=1, tiled=True)
    grad_attended = jnp.einsum(
        "td,fd->tf", cotangent_full, w_out, preferred_element_type=jnp.float32
    ).astype(jnp.bfloat16)
    grad_blocks = grad_attended.reshape(block_count, BLOCK_TILES, tile_rows, head_count, HEAD_DIM)
    resent = lax.all_to_all(
        select_pairs(local_pairs, incoming), "space", split_axis=1, concat_axis=1, tiled=True
    )
    backward_keys = jnp.concatenate(
        [local_pairs, resent.reshape(2, peer_count * slot_count, tile_rows, head_width)], 1
    )

    def backward_block(totals, triple):
        block_queries, block_entries, block_grads = triple
        keyset = gather_keys(backward_keys, block_entries, head_count)
        key_part = keyset[0]
        value_part = keyset[1]
        likely = probabilities(block_queries, key_part, score_scale)
        rounded = likely.astype(jnp.bfloat16)
        grad_prob = jnp.einsum(
            "bihe,bjhe->bhij", block_grads, value_part, preferred_element_type=jnp.float32
        )
        row_delta = jnp.sum(likely * grad_prob, axis=3, keepdims=True)
        grad_score = (likely * (grad_prob - row_delta) * score_scale).astype(jnp.bfloat16)
        grad_query = jnp.einsum(
            "bhij,bjhe->bihe", grad_score, key_part, preferred_element_type=jnp.float32
        )
        grad_key = jnp.einsum(
            "bhij,bihe->bjhe", grad_score, block_queries, preferred_element_type=jnp.float32
        )
        grad_value = jnp.einsum(
            "bhij,bihe->bjhe", rounded, block_grads, preferred_element_type=jnp.float32
        )
        entry_count = block_entries.shape[0] * NEIGHBOURS
        flat_entries = block_entries.reshape(-1)
        both_grads = jnp.stack(
            [grad_key.reshape(entry_count, -1), grad_value.reshape(entry_count, -1)], 0
        )
        return (totals.at[:, flat_entries].add(both_grads), grad_query)

    empty_total = jnp.zeros((2, extent, tile_rows * head_width), jnp.float32)
    pair_totals, query_grads = lax.scan(
        backward_block, empty_total, (queries, entries, grad_blocks)
    )
    near_part = pair_totals[:, :tile_count]
    far_part = (
        pair_totals[:, tile_count:]
        .astype(jnp.bfloat16)
        .reshape(2, peer_count, slot_count, tile_rows, head_width)
    )
    returned = lax.all_to_all(far_part, "space", split_axis=1, concat_axis=1, tiled=True)
    placer = (jnp.arange(tile_count, dtype=jnp.int32)[:, None] == incoming.reshape(1, -1)).astype(
        jnp.float32
    )
    landed = jnp.einsum(
        "tp,gpx->gtx",
        placer,
        returned.reshape(2, peer_count * slot_count, -1).astype(jnp.float32),
        precision=lax.Precision.HIGHEST,
    )
    pair_grads = (near_part + landed).reshape(2, row_count, head_width)
    grad_qkv = jnp.concatenate(
        [query_grads.reshape(1, row_count, head_width), pair_grads], 0
    ).astype(jnp.bfloat16)
    normed_rows = normed.T
    cotangent_rows = cotangent_full.T
    input_part = jnp.einsum(
        "ct,gtf->cgf", normed_rows, grad_qkv, preferred_element_type=jnp.float32
    )
    output_part = jnp.dot(cotangent_rows, attended, preferred_element_type=jnp.float32)
    stacked_grads = lax.psum_scatter(
        jnp.concatenate(
            [
                input_part.reshape(
                    model_width // peer_count * lax.axis_size("space"), 3 * head_width
                ),
                output_part,
            ],
            1,
        ).astype(jnp.bfloat16),
        "space",
        scatter_dimension=0,
        tiled=True,
    ).astype(jnp.float32)
    grad_w_qkv = stacked_grads[:, : 3 * head_width].reshape(-1, 3, head_width)
    grad_w_out = stacked_grads[:, 3 * head_width :].T
    grad_normed = jnp.einsum("gtf,dgf->td", grad_qkv, w_qkv, preferred_element_type=jnp.float32)
    own_standard = lax.dynamic_slice_in_dim(standard, column, col_share, 1)
    own_part = lax.psum_scatter(
        grad_normed.astype(jnp.bfloat16), "head", scatter_dimension=1, tiled=True
    ).astype(jnp.float32)
    row_sums = lax.psum(
        (jnp.sum(own_part, axis=1), jnp.sum(own_part * own_standard, axis=1)), "head"
    )
    first_mean = (row_sums[0] / model_width)[:, None]
    second_mean = (row_sums[1] / model_width)[:, None]
    cotangent_wide = cotangent.astype(jnp.float32)
    grad_tokens = (
        cotangent_wide + inverse * (own_part - first_mean - own_standard * second_mean)
    ).astype(jnp.bfloat16)
    return (layer_out, grad_tokens, grad_w_qkv, grad_w_out)


def solution(mesh):
    placed = (
        P("space", None),
        P(None, None, "head"),
        P("head", None),
        P("space", None),
        P("space", None, None),
        P("space", "head"),
    )
    return jax.shard_map(
        on_device,
        mesh=mesh,
        in_specs=placed,
        out_specs=(
            P("space", "head"),
            P("space", "head"),
            P("space", None, "head"),
            P("head", "space"),
        ),
        check_vma=False,
    )
```

profile of v0, /device:TPU:0, one launch (start us, length us, event | category | flops | bytes accessed | tf_op | source)
XLA Modules:
  0.0 916.5 jit_solution(7193930980082506994)
XLA Ops:
  60.7 36.5 %all-gather.2.cloned.1.call-done = bf16[1024,1024]{1,0:T(8,128)(2,1)} async-done(((bf16[1024,256]{1,0:T(8,128)(2,1)}), bf16[1024,1024]{1,0:T(8,128)(2,1)}) %all-gather.2.cloned.1.call-update) | async-done | bytes 2097168 | tf_op jit(solution)/shard_map/all_gather | solution.py:101
  100.5 64.0 %all-to-all-done.1 = bf16[2,32,2,128,256]{4,3,2,0,1:T(8,128)(2,1)} async-done(((bf16[2,32,2,128,256]{4,3,2,0,1:T(8,128)(2,1)}), bf16[2,32,2,128,256]{4,3,2,0,1:T(8,128)(2,1)}, u32[]{:S(2)}, u32[]{:S(2)}) %all-to-all-start.1) | async-done | bytes 8388640 | tf_op jit(solution)/shard_map/all_to_all | solution.py:77
  186.9 408.7 %while.23 = (s32[]{:T(128)}, f32[2,72,32768]{2,0,1:T(2,128)}, bf16[2,4,128,4,64]{2,4,3,1,0:T(8,128)(2,1)}, s32[2,4,9]{2,1,0:T(4,128)S(1)}, bf16[2,4,128,4,64]{2,...) while((s32[]{:T(128)}, f32[2,72,32768]{2,0,1:T(2,128)}, ...), condition=%wide.region_12.15_spmd, body=%wide.region_7.14_spmd.sunk | while | flops 1868574720 | bytes 270851232 | solution.py:142
  234.8 23.7 %fusion.197 = bf16[2,4,128,4,64]{2,4,3,1,0:T(8,128)(2,1)} fusion(bf16[2,4,128,4,64]{2,4,3,1,0:T(8,128)(2,1)} %get-tuple-element.308, s32[]{:T(128)S(6)} %copy.213, bf16[4,1152,4,64]{1,3,2,0:T(8,128)(2,1)S(1)} %copy-done.1, f32[4,4,128,1152]{3,2,1,0:T(8,128)} %fusion.195, f32[4,4,128,1152]{3,2,1,0:T(8,128)} %get-tuple-element.279, ...), kind=kOutput, calls=%fused_computation.52.clone.1 | convolution fusion | flops 318508160 | bytes 40648708 | tf_op jit(solution)/shard_map/while/body/eval_jaxpr/bhij,bjhe->bihe/dot_general | solution.py:125
  258.5 25.1 %fusion.196 = f32[4,1152,4,64]{1,3,2,0:T(8,128)} fusion(f32[4,4,128,1152]{3,2,1,0:T(8,128)} %fusion.195, bf16[2,4,128,4,64]{2,4,3,1,0:T(8,128)(2,1)} %get-tuple-element.318, s32[]{:T(128)S(6)} %copy.213, f32[4,4,128,1152]{3,2,1,0:T(8,128)} %get-tuple-element.279, f32[4,4,128]{2,1,0:T(4,128)S(1)} %get-tuple-element.277), kind=kOutput, calls=%fused_computation.50.clone.1 | convolution fusion | flops 318508160 | bytes 42745860 | tf_op jit(solution)/shard_map/while/body/eval_jaxpr/bhij,bihe->bjhe/dot_general | solution.py:128
  289.9 9.5 %copy.198 = f32[4,1152,4,64]{3,2,1,0:T(4,128)} copy(f32[4,1152,4,64]{1,3,2,0:T(8,128)} %fusion.194) | data formatting | bytes 9437184 | tf_op jit(solution)/shard_map/while/body/eval_jaxpr/bhij,bihe->bjhe/transpose | solution.py:131
  299.4 10.3 %reshape.263 = f32[1,36,32768]{2,1,0:T(8,128)} reshape(f32[4,1152,4,64]{3,2,1,0:T(4,128)} %copy.198) | data formatting | bytes 9437184 | tf_op jit(solution)/shard_map/while/body/eval_jaxpr/stack;while/body/eval_jaxpr/reshape | solution.py:136
  309.7 9.5 %copy.199 = f32[4,1152,4,64]{3,2,1,0:T(4,128)} copy(f32[4,1152,4,64]{1,3,2,0:T(8,128)} %fusion.196) | data formatting | bytes 9437184 | tf_op jit(solution)/shard_map/while/body/eval_jaxpr/bhij,bihe->bjhe/transpose | solution.py:128
  319.3 10.3 %reshape.265 = f32[1,36,32768]{2,1,0:T(8,128)} reshape(f32[4,1152,4,64]{3,2,1,0:T(4,128)} %copy.199) | data formatting | bytes 9437184 | tf_op jit(solution)/shard_map/while/body/eval_jaxpr/stack;while/body/eval_jaxpr/reshape | solution.py:136
  342.3 48.8 %scatter_fusion = f32[2,72,32768]{2,0,1:T(2,128)} fusion(f32[2,72,32768]{2,0,1:T(2,128)} %get-tuple-element.307, s32[36]{0:T(128)S(1)} %fusion.191, f32[36,2,32768]{2,1,0:T(2,128)} %copy.200), kind=kCustom, calls=%fused_computation.3.clone.1 | custom fusion | flops 2359296 | bytes 28311696 | tf_op jit(solution)/shard_map/while/body/eval_jaxpr/scatter-add | solution.py:139
  438.8 23.7 %fusion.197 = bf16[2,4,128,4,64]{2,4,3,1,0:T(8,128)(2,1)} fusion(bf16[2,4,128,4,64]{2,4,3,1,0:T(8,128)(2,1)} %get-tuple-element.308, s32[]{:T(128)S(6)} %copy.213, bf16[4,1152,4,64]{1,3,2,0:T(8,128)(2,1)S(1)} %copy-done.1, f32[4,4,128,1152]{3,2,1,0:T(8,128)} %fusion.195, f32[4,4,128,1152]{3,2,1,0:T(8,128)} %get-tuple-element.279, ...), kind=kOutput, calls=%fused_computation.52.clone.1 | convolution fusion | flops 318508160 | bytes 40648708 | tf_op jit(solution)/shard_map/while/body/eval_jaxpr/bhij,bjhe->bihe/dot_general | solution.py:125
  462.6 25.1 %fusion.196 = f32[4,1152,4,64]{1,3,2,0:T(8,128)} fusion(f32[4,4,128,1152]{3,2,1,0:T(8,128)} %fusion.195, bf16[2,4,128,4,64]{2,4,3,1,0:T(8,128)(2,1)} %get-tuple-element.318, s32[]{:T(128)S(6)} %copy.213, f32[4,4,128,1152]{3,2,1,0:T(8,128)} %get-tuple-element.279, f32[4,4,128]{2,1,0:T(4,128)S(1)} %get-tuple-element.277), kind=kOutput, calls=%fused_computation.50.clone.1 | convolution fusion | flops 318508160 | bytes 42745860 | tf_op jit(solution)/shard_map/while/body/eval_jaxpr/bhij,bihe->bjhe/dot_general | solution.py:128
  493.9 9.5 %copy.198 = f32[4,1152,4,64]{3,2,1,0:T(4,128)} copy(f32[4,1152,4,64]{1,3,2,0:T(8,128)} %fusion.194) | data formatting | bytes 9437184 | tf_op jit(solution)/shard_map/while/body/eval_jaxpr/bhij,bihe->bjhe/transpose | solution.py:131
  503.5 10.3 %reshape.263 = f32[1,36,32768]{2,1,0:T(8,128)} reshape(f32[4,1152,4,64]{3,2,1,0:T(4,128)} %copy.198) | data formatting | bytes 9437184 | tf_op jit(solution)/shard_map/while/body/eval_jaxpr/stack;while/body/eval_jaxpr/reshape | solution.py:136
  513.8 9.5 %copy.199 = f32[4,1152,4,64]{3,2,1,0:T(4,128)} copy(f32[4,1152,4,64]{1,3,2,0:T(8,128)} %fusion.196) | data formatting | bytes 9437184 | tf_op jit(solution)/shard_map/while/body/eval_jaxpr/bhij,bihe->bjhe/transpose | solution.py:128
  523.3 10.3 %reshape.265 = f32[1,36,32768]{2,1,0:T(8,128)} reshape(f32[4,1152,4,64]{3,2,1,0:T(4,128)} %copy.199) | data formatting | bytes 9437184 | tf_op jit(solution)/shard_map/while/body/eval_jaxpr/stack;while/body/eval_jaxpr/reshape | solution.py:136
  546.3 48.8 %scatter_fusion = f32[2,72,32768]{2,0,1:T(2,128)} fusion(f32[2,72,32768]{2,0,1:T(2,128)} %get-tuple-element.307, s32[36]{0:T(128)S(1)} %fusion.191, f32[36,2,32768]{2,1,0:T(2,128)} %copy.200), kind=kCustom, calls=%fused_computation.3.clone.1 | custom fusion | flops 2359296 | bytes 28311696 | tf_op jit(solution)/shard_map/while/body/eval_jaxpr/scatter-add | solution.py:139
  595.5 9.4 %slice.60 = bf16[2,64,32768]{2,0,1:T(2,128)(2,1)} slice(f32[2,72,32768]{2,0,1:T(2,128)} %get-tuple-element.73), slice={[0:2], [8:72], [0:32768]} | slice | bytes 16777216 | tf_op jit(solution)/shard_map/slice | solution.py:147
  604.9 14.0 %reshape.225 = bf16[2,32,2,128,256]{4,3,0,2,1:T(8,128)(2,1)} reshape(bf16[2,64,32768]{2,0,1:T(2,128)(2,1)} %slice.60) | data formatting | bytes 16777216 | tf_op jit(solution)/shard_map/reshape | solution.py:149
  631.9 85.3 %while.22 = (s32[]{:T(128)}, bf16[2,4,128,4,64]{2,1,0,4,3:T(4,128)(2,1)}, s32[2,4,9]{2,1,0:T(4,128)S(1)}, bf16[2,72,128,256]{3,2,1,0:T(8,128)(2,1)}, bf16[2,4,128,4,64]{2,4,3,1,0:T(8,128)(2,1)S(1)}, /*index=5*/s32[]{:T(128)}) while((s32[]{:T(128)}, bf16[2,4,128,4,64]{2,1,0,4,3:T(4,128)(2,1)}, s32[2,4,9]{2,1,0:T(4,128)S(1)}, ...), condition=%wide.region_5.8_spmd, body=%wide.region_2.7_spmd.sunk | while | flops 618269120 | bytes 66606568 | solution.py:94
  720.8 18.2 %copy.135 = f32[2,72,32768]{2,1,0:T(8,128)} copy(f32[2,72,32768]{2,0,1:T(2,128)} %get-tuple-element.73) | data formatting | bytes 37748736 | tf_op jit(solution)/shard_map/while | solution.py:142
  750.0 13.5 %reshape.172 = bf16[2,64,32768]{2,1,0:T(8,128)(2,1)} reshape(bf16[2,32,2,128,256]{4,3,2,1,0:T(8,128)(2,1)} %copy.138) | data formatting | bytes 16777216 | tf_op jit(solution)/shard_map/reshape | solution.py:158
  794.3 71.0 %reduce-scatter.8.cloned.1.call-done = bf16[32,1024]{1,0:T(8,128)(2,1)} async-done(((bf16[1024,1024]{1,0:T(8,128)(2,1)}), bf16[32,1024]{1,0:T(8,128)(2,1)}) %reduce-scatter.8.cloned.1.call-update) | async-done | bytes 65552 | tf_op jit(solution)/shard_map/reduce_scatter | solution.py:171
  868.2 28.4 %reduce-scatter.6.cloned.1.call-done = bf16[1024,256]{1,0:T(8,128)(2,1)} async-done(((bf16[1024,1024]{1,0:T(8,128)(2,1)}), bf16[1024,256]{1,0:T(8,128)(2,1)}) %reduce-scatter.6.cloned.1.call-update) | async-done | bytes 524304 | tf_op jit(solution)/shard_map/reduce_scatter | solution.py:189
  (174 shorter events, 371.8 us)
Async XLA Ops:
  7.2 90.0 %copy-start = (bf16[256,1024]{1,0:T(8,128)(2,1)S(1)}, bf16[256,1024]{1,0:T(8,128)(2,1)}, u32[]{:S(2)}) copy-start(bf16[256,1024]{1,0:T(8,128)(2,1)} %param.16) | copy-start | bytes 1572868
  7.2 16.6 %copy-start.2 = (bf16[1024,1024]{1,0:T(8,128)(2,1)S(1)}, bf16[1024,1024]{1,0:T(8,128)(2,1)}, u32[]{:S(2)}) copy-start(bf16[1024,1024]{1,0:T(8,128)(2,1)} %param.14) | copy-start | bytes 6291460
  8.7 20.2 %all-to-all-start = ((s32[32,1,2]{2,1,0:T(1,128)}), s32[32,1,2]{2,1,0:T(1,128)S(1)}, u32[]{:S(2)}, u32[]{:S(2)}) async-start(s32[32,1,2]{2,1,0:T(1,128)} %copy.125), calls=%async_computation | async-start | bytes 32768 | tf_op jit(solution)/shard_map/all_to_all | solution.py:72
  18.9 8.3 copy-start.13
  21.2 6.0 copy-start.11
  30.2 5.4 copy-start.15
  50.9 8.4 slice-start
  51.0 113.5 %all-to-all-start.1 = ((bf16[2,32,2,128,256]{4,3,2,0,1:T(8,128)(2,1)}), bf16[2,32,2,128,256]{4,3,2,0,1:T(8,128)(2,1)}, u32[]{:S(2)}, u32[]{:S(2)}) async-start(bf16[2,32,2,128,256]{4,3,2,0,1:T(8,128)(2,1)} %copy.127), calls=%async_computation.1 | async-start | bytes 16777216 | tf_op jit(solution)/shard_map/all_to_all | solution.py:77
  58.6 38.6 %all-gather.2.cloned.1.call-start = ((), (), s32[]{:S(2)}) async-start(), calls=%async_computation.7 | async-start | bytes 2621440 | tf_op jit(solution)/shard_map/all_gather | solution.py:101
  180.1 6.7 copy-start.10
  219.7 7.8 copy-start.1
  423.8 7.8 copy-start.1
  626.7 115.5 %all-to-all-start.2 = ((bf16[2,32,2,128,256]{4,3,2,0,1:T(8,128)(2,1)}), bf16[2,32,2,128,256]{4,3,2,0,1:T(8,128)(2,1)}, u32[]{:S(2)}, u32[]{:S(2)}) async-start(bf16[2,32,2,128,256]{4,3,2,0,1:T(8,128)(2,1)} %copy.137), calls=%async_computation.3 | async-start | bytes 16777216 | tf_op jit(solution)/shard_map/all_to_all | solution.py:151
  631.8 160.5 %reduce-scatter.4.cloned.1.call-start = ((), (), s32[]{:S(2)}) async-start(), calls=%async_computation.6 | async-start | bytes 2621440 | tf_op jit(solution)/shard_map/reduce_scatter | solution.py:96
  666.3 7.2 copy-start.8
  708.9 7.2 copy-start.8
  720.7 144.6 %reduce-scatter.8.cloned.1.call-start = ((), (), s32[]{:S(2)}) async-start(), calls=%async_computation.9 | async-start | bytes 2162688 | tf_op jit(solution)/shard_map/reduce_scatter | solution.py:171
  720.8 18.2 %copy-start.17 = (bf16[1024,1024]{1,0:T(8,128)(2,1)S(1)}, bf16[1024,1024]{1,0:T(8,128)(2,1)}, u32[]{:S(2)}) copy-start(bf16[1024,1024]{1,0:T(8,128)(2,1)} %all-gather.2.cloned.1.call-done) | copy-start | bytes 6291460
  750.0 13.5 %copy-start.16 = (s32[64]{0:T(128)S(1)}, s32[64]{0:T(128)}, u32[]{:S(2)}) copy-start(s32[64]{0:T(128)} %copy-done.15) | copy-start | bytes 772
  763.5 10.9 %copy-start.3 = (bf16[1024,1024]{1,0:T(8,128)(2,1)S(1)}, bf16[1024,1024]{1,0:T(8,128)(2,1)}, u32[]{:S(2)}) copy-start(bf16[1024,1024]{1,0:T(8,128)(2,1)} %param.14) | copy-start | bytes 6291460
  763.5 10.9 %copy-start.12 = (f32[1024]{0:T(1024)S(1)}, f32[1024]{0:T(1024)}, u32[]{:S(2)}) copy-start(f32[1024]{0:T(1024)} %copy-done.11) | copy-start | bytes 12292
  763.5 10.9 %copy-start.14 = (f32[1024]{0:T(1024)S(1)}, f32[1024]{0:T(1024)}, u32[]{:S(2)}) copy-start(f32[1024]{0:T(1024)} %copy-done.13) | copy-start | bytes 12292
  784.7 112.0 %reduce-scatter.6.cloned.1.call-start = ((), (), s32[]{:S(2)}) async-start(), calls=%async_computation.8 | async-start | bytes 2621440 | tf_op jit(solution)/shard_map/reduce_scatter | solution.py:189
  789.9 117.3 %copy-start.5 = (bf16[1024,256]{1,0:T(8,128)(2,1)S(1)}, bf16[1024,256]{1,0:T(8,128)(2,1)}, u32[]{:S(2)}) copy-start(bf16[1024,256]{1,0:T(8,128)(2,1)} %param.19) | copy-start | bytes 1572868
  (5 other events, 9.0 us)
Sparse Core Ops, SparseCore 0:
  61.1 36.0 all-gather.1
  720.8 31.2 reduce-scatter.3
  784.8 80.4 reduce-scatter.7
  867.7 28.9 reduce-scatter.5
where the time goes:
time: 930 us; the launch traced here: 917 us
  local copies, waits for them, and re-layouts  322 us (35%)
  waiting for transfers between devices  201 us (22%)
  matrix products  198 us (21%)
  other arithmetic  152 us (16%)
  starting transfers between devices  21.2 us (2%)
  between operations  14.3 us (2%)
    scatter-add x2, other arithmetic, backward_block(): return (totals.at[:, flat_entries].add(both_grads), grad_query)  97.6 us
    reduce_scatter x1, waiting for transfers between devices, on_device(): lax.psum_scatter(jnp.concatenate([input_part.reshape(model_width // peer_...  71 us
    all_to_all x1, waiting for transfers between devices, on_device(): lax.all_to_all(outgoing, 'space', split_axis=1, concat_axis=1, tiled=True)  64 us
    dot_general x2, matrix products, backward_block(): jnp.einsum('bhij,bihe->bjhe', grad_score, block_queries, preferred_elemen...  50.2 us
    dot_general x2, matrix products, backward_block(): jnp.einsum('bhij,bjhe->bihe', grad_score, key_part, preferred_element_typ...  47.5 us
    reshape x4, local copies, waits for them, and re-layouts, backward_block(): jnp.stack([grad_key.reshape(entry_count, -1), grad_value.reshape(entry_co...  41.3 us
    all_gather x1, waiting for transfers between devices, on_device(): cotangent_full = lax.all_gather(cotangent, 'head', axis=1, tiled=True)  36.5 us
    sub x4, matrix products, probabilities(): weights = jnp.exp(scores - row_top)  33.2 us
  transfers between devices with their start and end apart: 7, of which 4 were waited for; matrix products, arithmetic and copies ran while one was open for 19% of the time, Pallas kernels for 0%

commit v1 on v0

--- a/solution.py
+++ b/solution.py
@@ -98,7 +98,18 @@
     ).astype(jnp.float32)
     own_tokens = lax.dynamic_slice_in_dim(tokens, column, col_share, 1).astype(jnp.float32)
     layer_out = (own_tokens + summed).astype(jnp.bfloat16)
-    cotangent_full = lax.all_gather(cotangent, "head", axis=1, tiled=True)
+    ways = lax.axis_size("head")
+    up = [(d, (d + 1) % ways) for d in range(ways)]
+    down = [(d, (d - 1) % ways) for d in range(ways)]
+    earlier, later = ([cotangent], [cotangent])
+    for _ in range(ways // 2):
+        earlier.append(lax.ppermute(earlier[-1], "head", up))
+    for _ in range((ways - 1) // 2):
+        later.append(lax.ppermute(later[-1], "head", down))
+    line = jnp.concatenate([*earlier[::-1], *later[1:]], axis=1)
+    cotangent_full = jnp.roll(
+        line, (lax.axis_index("head") - ways // 2) * cotangent.shape[1], axis=1
+    )
     grad_attended = jnp.einsum(
         "td,fd->tf", cotangent_full, w_out, preferred_element_type=jnp.float32
     ).astype(jnp.bfloat16)

time: 930 us -> 929 us (level)
  waiting for transfers between devices: 201 us -> 188 us
    all_gather x1 -> x0, waiting for transfers between devices: 36.5 us -> none  [on_device(): cotangent_full = lax.all_gather(cotangent, 'head', axis=1, tiled=True)]
    ppermute x0 -> x3, waiting for transfers between devices: none -> 18.7 us  [the longest x2 18.7 us: on_device(): earlier.append(lax.ppermute(earlier[-1], 'head', up))]
  transfers between devices with their start and end apart: 7 -> 9, of which waited for: 4 -> 5; matrix products, arithmetic and copies ran while one was open for 19% -> 20% of each run, Pallas kernels for 0% -> 0%
where the time goes in v1:
time: 929 us; the launch traced here: 917 us
  local copies, waits for them, and re-layouts  331 us (36%)
  matrix products  196 us (21%)
  waiting for transfers between devices  188 us (20%)
  other arithmetic  152 us (16%)
  starting transfers between devices  26.5 us (3%)
  between operations  14.3 us (2%)
    scatter-add x2, other arithmetic, backward_block(): return (totals.at[:, flat_entries].add(both_grads), grad_query)  97.6 us
    reduce_scatter x1, waiting for transfers between devices, on_device(): lax.psum_scatter(jnp.concatenate([input_part.reshape(model_width // peer_...  71.1 us
    all_to_all x1, waiting for transfers between devices, on_device(): lax.all_to_all(outgoing, 'space', split_axis=1, concat_axis=1, tiled=True)  69.4 us
    dot_general x2, matrix products, backward_block(): jnp.einsum('bhij,bihe->bjhe', grad_score, block_queries, preferred_elemen...  50.2 us
    dot_general x2, matrix products, backward_block(): jnp.einsum('bhij,bjhe->bihe', grad_score, key_part, preferred_element_typ...  47.5 us
    reshape x4, local copies, waits for them, and re-layouts, backward_block(): jnp.stack([grad_key.reshape(entry_count, -1), grad_value.reshape(entry_co...  41.3 us
    sub x4, matrix products, probabilities(): weights = jnp.exp(scores - row_top)  33.2 us
    gather x4, local copies, waits for them, and re-layouts, gather_keys(): picked = jnp.take(extended, block_entries.reshape(-1), axis=1)  32.9 us
  transfers between devices with their start and end apart: 9, of which 5 were waited for; matrix products, arithmetic and copies ran while one was open for 20% of the time, Pallas kernels for 0%

profile of v1, /device:TPU:0, one launch (start us, length us, event | category | flops | bytes accessed | tf_op | source)
XLA Modules:
  0.0 916.8 jit_solution(10625234154134708913)
XLA Ops:
  60.3 13.7 %collective-permute-done = bf16[1024,256]{1,0:T(8,128)(2,1)S(1)} collective-permute-done((bf16[1024,256]{1,0:T(8,128)(2,1)S(1)}, bf16[1024,256]{1,0:T(8,128)(2,1)S(1)}, u32[]{:S(2)}, u32[]{:S(2)}) %collective-permute-start) | collective-permute-done | bytes 524320 | tf_op jit(solution)/shard_map/ppermute | solution.py:106
  95.1 69.4 %all-to-all-done.1 = bf16[2,32,2,128,256]{4,3,2,0,1:T(8,128)(2,1)} async-done(((bf16[2,32,2,128,256]{4,3,2,0,1:T(8,128)(2,1)}), bf16[2,32,2,128,256]{4,3,2,0,1:T(8,128)(2,1)}, u32[]{:S(2)}, u32[]{:S(2)}) %all-to-all-start.1) | async-done | bytes 8388640 | tf_op jit(solution)/shard_map/all_to_all | solution.py:77
  186.9 408.7 %while.23 = (s32[]{:T(128)}, f32[2,72,32768]{2,0,1:T(2,128)}, bf16[2,4,128,4,64]{2,4,3,1,0:T(8,128)(2,1)}, s32[2,4,9]{2,1,0:T(4,128)S(1)}, bf16[2,4,128,4,64]{2,...) while((s32[]{:T(128)}, f32[2,72,32768]{2,0,1:T(2,128)}, ...), condition=%wide.region_12.15_spmd, body=%wide.region_7.14_spmd.sunk | while | flops 1868574720 | bytes 270851232 | solution.py:153
  234.8 23.7 %fusion.206 = bf16[2,4,128,4,64]{2,4,3,1,0:T(8,128)(2,1)} fusion(bf16[2,4,128,4,64]{2,4,3,1,0:T(8,128)(2,1)} %get-tuple-element.308, s32[]{:T(128)S(6)} %copy.220, bf16[4,1152,4,64]{1,3,2,0:T(8,128)(2,1)S(1)} %copy-done.1, f32[4,4,128,1152]{3,2,1,0:T(8,128)} %fusion.204, f32[4,4,128,1152]{3,2,1,0:T(8,128)} %get-tuple-element.279, ...), kind=kOutput, calls=%fused_computation.52.clone.1 | convolution fusion | flops 318508160 | bytes 40648708 | tf_op jit(solution)/shard_map/while/body/eval_jaxpr/bhij,bjhe->bihe/dot_general | solution.py:136
  258.5 25.1 %fusion.205 = f32[4,1152,4,64]{1,3,2,0:T(8,128)} fusion(f32[4,4,128,1152]{3,2,1,0:T(8,128)} %fusion.204, bf16[2,4,128,4,64]{2,4,3,1,0:T(8,128)(2,1)} %get-tuple-element.318, s32[]{:T(128)S(6)} %copy.220, f32[4,4,128,1152]{3,2,1,0:T(8,128)} %get-tuple-element.279, f32[4,4,128]{2,1,0:T(4,128)S(1)} %get-tuple-element.277), kind=kOutput, calls=%fused_computation.50.clone.1 | convolution fusion | flops 318508160 | bytes 42745860 | tf_op jit(solution)/shard_map/while/body/eval_jaxpr/bhij,bihe->bjhe/dot_general | solution.py:139
  289.9 9.5 %copy.198 = f32[4,1152,4,64]{3,2,1,0:T(4,128)} copy(f32[4,1152,4,64]{1,3,2,0:T(8,128)} %fusion.203) | data formatting | bytes 9437184 | tf_op jit(solution)/shard_map/while/body/eval_jaxpr/bhij,bihe->bjhe/transpose | solution.py:142
  299.4 10.3 %reshape.263 = f32[1,36,32768]{2,1,0:T(8,128)} reshape(f32[4,1152,4,64]{3,2,1,0:T(4,128)} %copy.198) | data formatting | bytes 9437184 | tf_op jit(solution)/shard_map/while/body/eval_jaxpr/stack;while/body/eval_jaxpr/reshape | solution.py:147
  309.7 9.5 %copy.199 = f32[4,1152,4,64]{3,2,1,0:T(4,128)} copy(f32[4,1152,4,64]{1,3,2,0:T(8,128)} %fusion.205) | data formatting | bytes 9437184 | tf_op jit(solution)/shard_map/while/body/eval_jaxpr/bhij,bihe->bjhe/transpose | solution.py:139
  319.3 10.3 %reshape.265 = f32[1,36,32768]{2,1,0:T(8,128)} reshape(f32[4,1152,4,64]{3,2,1,0:T(4,128)} %copy.199) | data formatting | bytes 9437184 | tf_op jit(solution)/shard_map/while/body/eval_jaxpr/stack;while/body/eval_jaxpr/reshape | solution.py:147
  342.3 48.8 %scatter_fusion = f32[2,72,32768]{2,0,1:T(2,128)} fusion(f32[2,72,32768]{2,0,1:T(2,128)} %get-tuple-element.307, s32[36]{0:T(128)S(1)} %fusion.200, f32[36,2,32768]{2,1,0:T(2,128)} %copy.200), kind=kCustom, calls=%fused_computation.3.clone.1 | custom fusion | flops 2359296 | bytes 28311696 | tf_op jit(solution)/shard_map/while/body/eval_jaxpr/scatter-add | solution.py:150
  438.8 23.7 %fusion.206 = bf16[2,4,128,4,64]{2,4,3,1,0:T(8,128)(2,1)} fusion(bf16[2,4,128,4,64]{2,4,3,1,0:T(8,128)(2,1)} %get-tuple-element.308, s32[]{:T(128)S(6)} %copy.220, bf16[4,1152,4,64]{1,3,2,0:T(8,128)(2,1)S(1)} %copy-done.1, f32[4,4,128,1152]{3,2,1,0:T(8,128)} %fusion.204, f32[4,4,128,1152]{3,2,1,0:T(8,128)} %get-tuple-element.279, ...), kind=kOutput, calls=%fused_computation.52.clone.1 | convolution fusion | flops 318508160 | bytes 40648708 | tf_op jit(solution)/shard_map/while/body/eval_jaxpr/bhij,bjhe->bihe/dot_general | solution.py:136
  462.6 25.1 %fusion.205 = f32[4,1152,4,64]{1,3,2,0:T(8,128)} fusion(f32[4,4,128,1152]{3,2,1,0:T(8,128)} %fusion.204, bf16[2,4,128,4,64]{2,4,3,1,0:T(8,128)(2,1)} %get-tuple-element.318, s32[]{:T(128)S(6)} %copy.220, f32[4,4,128,1152]{3,2,1,0:T(8,128)} %get-tuple-element.279, f32[4,4,128]{2,1,0:T(4,128)S(1)} %get-tuple-element.277), kind=kOutput, calls=%fused_computation.50.clone.1 | convolution fusion | flops 318508160 | bytes 42745860 | tf_op jit(solution)/shard_map/while/body/eval_jaxpr/bhij,bihe->bjhe/dot_general | solution.py:139
  493.9 9.5 %copy.198 = f32[4,1152,4,64]{3,2,1,0:T(4,128)} copy(f32[4,1152,4,64]{1,3,2,0:T(8,128)} %fusion.203) | data formatting | bytes 9437184 | tf_op jit(solution)/shard_map/while/body/eval_jaxpr/bhij,bihe->bjhe/transpose | solution.py:142
  503.5 10.3 %reshape.263 = f32[1,36,32768]{2,1,0:T(8,128)} reshape(f32[4,1152,4,64]{3,2,1,0:T(4,128)} %copy.198) | data formatting | bytes 9437184 | tf_op jit(solution)/shard_map/while/body/eval_jaxpr/stack;while/body/eval_jaxpr/reshape | solution.py:147
  513.8 9.5 %copy.199 = f32[4,1152,4,64]{3,2,1,0:T(4,128)} copy(f32[4,1152,4,64]{1,3,2,0:T(8,128)} %fusion.205) | data formatting | bytes 9437184 | tf_op jit(solution)/shard_map/while/body/eval_jaxpr/bhij,bihe->bjhe/transpose | solution.py:139
  523.3 10.3 %reshape.265 = f32[1,36,32768]{2,1,0:T(8,128)} reshape(f32[4,1152,4,64]{3,2,1,0:T(4,128)} %copy.199) | data formatting | bytes 9437184 | tf_op jit(solution)/shard_map/while/body/eval_jaxpr/stack;while/body/eval_jaxpr/reshape | solution.py:147
  546.3 48.8 %scatter_fusion = f32[2,72,32768]{2,0,1:T(2,128)} fusion(f32[2,72,32768]{2,0,1:T(2,128)} %get-tuple-element.307, s32[36]{0:T(128)S(1)} %fusion.200, f32[36,2,32768]{2,1,0:T(2,128)} %copy.200), kind=kCustom, calls=%fused_computation.3.clone.1 | custom fusion | flops 2359296 | bytes 28311696 | tf_op jit(solution)/shard_map/while/body/eval_jaxpr/scatter-add | solution.py:150
  595.5 9.4 %slice.60 = bf16[2,64,32768]{2,0,1:T(2,128)(2,1)} slice(f32[2,72,32768]{2,0,1:T(2,128)} %get-tuple-element.73), slice={[0:2], [8:72], [0:32768]} | slice | bytes 16777216 | tf_op jit(solution)/shard_map/slice | solution.py:158
  604.9 14.0 %reshape.225 = bf16[2,32,2,128,256]{4,3,0,2,1:T(8,128)(2,1)} reshape(bf16[2,64,32768]{2,0,1:T(2,128)(2,1)} %slice.60) | data formatting | bytes 16777216 | tf_op jit(solution)/shard_map/reshape | solution.py:160
  631.9 85.4 %while.22 = (s32[]{:T(128)}, bf16[2,4,128,4,64]{2,1,0,4,3:T(4,128)(2,1)}, s32[2,4,9]{2,1,0:T(4,128)S(1)}, bf16[2,72,128,256]{3,2,1,0:T(8,128)(2,1)}, bf16[2,4,128,4,64]{2,4,3,1,0:T(8,128)(2,1)S(1)}, /*index=5*/s32[]{:T(128)}) while((s32[]{:T(128)}, bf16[2,4,128,4,64]{2,1,0,4,3:T(4,128)(2,1)}, s32[2,4,9]{2,1,0:T(4,128)S(1)}, ...), condition=%wide.region_5.8_spmd, body=%wide.region_2.7_spmd.sunk | while | flops 618269120 | bytes 66606568 | solution.py:94
  720.9 18.2 %copy.135 = f32[2,72,32768]{2,1,0:T(8,128)} copy(f32[2,72,32768]{2,0,1:T(2,128)} %get-tuple-element.73) | data formatting | bytes 37748736 | tf_op jit(solution)/shard_map/while | solution.py:153
  750.2 13.5 %reshape.172 = bf16[2,64,32768]{2,1,0:T(8,128)(2,1)} reshape(bf16[2,32,2,128,256]{4,3,2,1,0:T(8,128)(2,1)} %copy.138) | data formatting | bytes 16777216 | tf_op jit(solution)/shard_map/reshape | solution.py:169
  794.4 71.1 %reduce-scatter.8.cloned.1.call-done = bf16[32,1024]{1,0:T(8,128)(2,1)} async-done(((bf16[1024,1024]{1,0:T(8,128)(2,1)}), bf16[32,1024]{1,0:T(8,128)(2,1)}) %reduce-scatter.8.cloned.1.call-update) | async-done | bytes 65552 | tf_op jit(solution)/shard_map/reduce_scatter | solution.py:182
  868.4 28.6 %reduce-scatter.6.cloned.1.call-done = bf16[1024,256]{1,0:T(8,128)(2,1)} async-done(((bf16[1024,1024]{1,0:T(8,128)(2,1)}), bf16[1024,256]{1,0:T(8,128)(2,1)}) %reduce-scatter.6.cloned.1.call-update) | async-done | bytes 524304 | tf_op jit(solution)/shard_map/reduce_scatter | solution.py:200
  (188 shorter events, 389.2 us)
Async XLA Ops:
  7.2 86.2 %copy-start = (bf16[256,1024]{1,0:T(8,128)(2,1)S(1)}, bf16[256,1024]{1,0:T(8,128)(2,1)}, u32[]{:S(2)}) copy-start(bf16[256,1024]{1,0:T(8,128)(2,1)} %param.16) | copy-start | bytes 1572868
  7.2 16.6 %copy-start.2 = (bf16[1024,1024]{1,0:T(8,128)(2,1)S(1)}, bf16[1024,1024]{1,0:T(8,128)(2,1)}, u32[]{:S(2)}) copy-start(bf16[1024,1024]{1,0:T(8,128)(2,1)} %param.14) | copy-start | bytes 6291460
  8.7 20.2 %all-to-all-start = ((s32[32,1,2]{2,1,0:T(1,128)}), s32[32,1,2]{2,1,0:T(1,128)S(1)}, u32[]{:S(2)}, u32[]{:S(2)}) async-start(s32[32,1,2]{2,1,0:T(1,128)} %copy.125), calls=%async_computation | async-start | bytes 32768 | tf_op jit(solution)/shard_map/all_to_all | solution.py:72
  18.9 8.3 copy-start.16
  50.9 7.7 copy-start.4
  51.0 113.5 %all-to-all-start.1 = ((bf16[2,32,2,128,256]{4,3,2,0,1:T(8,128)(2,1)}), bf16[2,32,2,128,256]{4,3,2,0,1:T(8,128)(2,1)}, u32[]{:S(2)}, u32[]{:S(2)}) async-start(bf16[2,32,2,128,256]{4,3,2,0,1:T(8,128)(2,1)} %copy.127), calls=%async_computation.1 | async-start | bytes 16777216 | tf_op jit(solution)/shard_map/all_to_all | solution.py:77
  58.6 15.4 %collective-permute-start = (bf16[1024,256]{1,0:T(8,128)(2,1)S(1)}, bf16[1024,256]{1,0:T(8,128)(2,1)S(1)}, u32[]{:S(2)}, u32[]{:S(2)}) collective-permute-start(bf16[1024,256]{1,0:T(8,128)(2,1)S(1)} %copy-done.4), channel_id=1, source_target_pairs={{0,1},{1,2},{2,3},{3,0},{4,5},{5,6},{6,7},{7,4},{8,9},{9,10},{10,1... | collective-permute-start | bytes 1572872 | tf_op jit(solution)/shard_map/ppermute | solution.py:106
  74.0 14.7 %collective-permute-start.1 = (bf16[1024,256]{1,0:T(8,128)(2,1)S(1)}, bf16[1024,256]{1,0:T(8,128)(2,1)}, u32[]{:S(2)}, u32[]{:S(2)}) collective-permute-start(bf16[1024,256]{1,0:T(8,128)(2,1)S(1)} %collective-permute-done), channel_id=1, source_target_pairs={{0,1},{1,2},{2,3},{3,0},{4,5},{5,6},{6,7},{7,4},{8,9},{9,10},{10,1... | collective-permute-start | bytes 1572872 | tf_op jit(solution)/shard_map/ppermute | solution.py:106
  74.3 15.6 %collective-permute-start.2 = (bf16[1024,256]{1,0:T(8,128)(2,1)S(1)}, bf16[1024,256]{1,0:T(8,128)(2,1)S(1)}, u32[]{:S(2)}, u32[]{:S(2)}) collective-permute-start(bf16[1024,256]{1,0:T(8,128)(2,1)S(1)} %copy-done.4), channel_id=1, source_target_pairs={{0,3},{1,0},{2,1},{3,2},{4,7},{5,4},{6,5},{7,6},{8,11},{9,8},{10,9... | collective-permute-start | bytes 1572872 | tf_op jit(solution)/shard_map/ppermute | solution.py:108
  180.1 6.7 copy-start.11
  219.7 7.8 copy-start.1
  423.8 7.8 copy-start.1
  626.7 115.6 %all-to-all-start.2 = ((bf16[2,32,2,128,256]{4,3,2,0,1:T(8,128)(2,1)}), bf16[2,32,2,128,256]{4,3,2,0,1:T(8,128)(2,1)}, u32[]{:S(2)}, u32[]{:S(2)}) async-start(bf16[2,32,2,128,256]{4,3,2,0,1:T(8,128)(2,1)} %copy.137), calls=%async_computation.3 | async-start | bytes 16777216 | tf_op jit(solution)/shard_map/all_to_all | solution.py:162
  631.8 160.6 %reduce-scatter.4.cloned.1.call-start = ((), (), s32[]{:S(2)}) async-start(), calls=%async_computation.6 | async-start | bytes 2621440 | tf_op jit(solution)/shard_map/reduce_scatter | solution.py:96
  666.3 7.2 copy-start.9
  709.0 7.2 copy-start.9
  720.8 144.7 %reduce-scatter.8.cloned.1.call-start = ((), (), s32[]{:S(2)}) async-start(), calls=%async_computation.8 | async-start | bytes 2162688 | tf_op jit(solution)/shard_map/reduce_scatter | solution.py:182
  720.8 18.2 %copy-start.13 = (bf16[1024,2048]{1,0:T(8,128)(2,1)S(1)}, bf16[1024,2048]{1,0:T(8,128)(2,1)}, u32[]{:S(2)}) copy-start(bf16[1024,2048]{1,0:T(8,128)(2,1)} %copy-done.12) | copy-start | bytes 12582916
  750.2 13.5 %copy-start.19 = (s32[64]{0:T(128)S(1)}, s32[64]{0:T(128)}, u32[]{:S(2)}) copy-start(s32[64]{0:T(128)} %copy-done.18) | copy-start | bytes 772
  763.7 10.9 %copy-start.3 = (bf16[1024,1024]{1,0:T(8,128)(2,1)S(1)}, bf16[1024,1024]{1,0:T(8,128)(2,1)}, u32[]{:S(2)}) copy-start(bf16[1024,1024]{1,0:T(8,128)(2,1)} %param.14) | copy-start | bytes 6291460
  763.7 10.9 %copy-start.15 = (f32[1024]{0:T(1024)S(1)}, f32[1024]{0:T(1024)}, u32[]{:S(2)}) copy-start(f32[1024]{0:T(1024)} %copy-done.14) | copy-start | bytes 12292
  763.7 10.9 %copy-start.17 = (f32[1024]{0:T(1024)S(1)}, f32[1024]{0:T(1024)}, u32[]{:S(2)}) copy-start(f32[1024]{0:T(1024)} %copy-done.16) | copy-start | bytes 12292
  784.9 112.1 %reduce-scatter.6.cloned.1.call-start = ((), (), s32[]{:S(2)}) async-start(), calls=%async_computation.7 | async-start | bytes 2621440 | tf_op jit(solution)/shard_map/reduce_scatter | solution.py:200
  790.0 117.5 %copy-start.5 = (bf16[1024,256]{1,0:T(8,128)(2,1)S(1)}, bf16[1024,256]{1,0:T(8,128)(2,1)}, u32[]{:S(2)}) copy-start(bf16[1024,256]{1,0:T(8,128)(2,1)} %param.19) | copy-start | bytes 1572868
  (8 other events, 22.3 us)
Sparse Core Ops, SparseCore 0:
  720.9 31.2 reduce-scatter.3
  785.0 80.4 reduce-scatter.7
  868.0 28.9 reduce-scatter.5
